TPU v7x, 512 devices: a whole 4x8x8 slice. The times are simulated.
512 devices in a mesh: frame: 32 (over x, y_lo, core), patch: 16 (over y_hi, z).
Axes of the slice: x: 4, y: 8 (y_hi: 2, y_lo: 4; y = y_hi * 4 + y_lo), z: 8, core: 2. Of those that a mesh axis runs over, the one named last changes fastest.
Arguments:
- latents: bfloat16 [32, 48, 128, 320], P('frame', 'patch'), may hold values from -6 to 6
- stale_kv: bfloat16 [32, 48, 128, 640], P('frame', 'patch'), may hold values from -8 to 8
- frame_ids: int32 [32], replicated, may hold values from 0 to 63
- timestep: int32 [1], replicated, may hold values from 0 to 999
- conv_weight: bfloat16 [3, 3, 320, 320], replicated, may hold values from -0.109375 to 0.109375
- time_proj: bfloat16 [320, 320], replicated, may hold values from -0.3125 to 0.3125
- spatial_qkv: bfloat16 [320, 960], replicated, may hold values from -0.4472136 to 0.4472136
- spatial_out: bfloat16 [320, 320], replicated, may hold values from -0.3125 to 0.3125
- temporal_qkv: bfloat16 [320, 960], replicated, may hold values from -0.3125 to 0.3125
- temporal_out: bfloat16 [320, 320], replicated, may hold values from -0.3125 to 0.3125
- frame_table: bfloat16 [64, 320], replicated, may hold values from -6 to 6
Outputs:
- result: bfloat16 [32, 48, 128, 320], P('frame', 'patch')
- fresh_kv: bfloat16 [32, 48, 128, 640], P('frame', 'patch')
All inputs are finite; a program needn't handle non-finite values.
Results may differ from a plain program's by a relative error of at most 0.011.
Values may be sent and summed in bfloat16 or wider, within the bound.
A program may use at most 64 MiB of HBM per device.

v0:
```python
import math

import jax
import jax.numpy as jnp
from jax import lax
from jax.sharding import PartitionSpec as P

HEADS = 5
GROUPS = 32


def extended(block, sides, width):
    for axis, dim in sides:
        count = lax.axis_size(axis)
        forward = [(i, i + 1) for i in range(count - 1)]
        backward = [(target, source) for source, target in forward]
        low = lax.ppermute(
            lax.slice_in_dim(block, block.shape[dim] - width, None, axis=dim), axis, forward
        )
        high = lax.ppermute(lax.slice_in_dim(block, 0, width, axis=dim), axis, backward)
        block = jnp.concatenate([low, block, high], axis=dim)
    return block


def layer_norm(values):
    centre = values - jnp.mean(values, axis=-1, keepdims=True)
    spread = jnp.mean(centre * centre, axis=-1, keepdims=True)
    return centre * lax.rsqrt(spread + 1e-05)


def attend(carry, queries, keys, values, valid):
    peak_old, total_old, summed_old = carry
    head_dim = queries.shape[-1]
    scores = jnp.einsum(
        "fqhd,fkhd->fhqk", queries, keys, preferred_element_type=jnp.float32
    ) / math.sqrt(head_dim)
    peak_new = jnp.where(valid, jnp.maximum(peak_old, jnp.max(scores, axis=-1)), peak_old)
    weights = jnp.where(valid, jnp.exp(scores - peak_new[..., None]), 0.0)
    factor = jnp.exp(peak_old - peak_new)
    total_new = total_old * factor + jnp.sum(weights, axis=-1)
    summed = jnp.einsum(
        "fhqk,fkhd->fqhd", weights.astype(jnp.bfloat16), values, preferred_element_type=jnp.float32
    )
    summed_new = summed_old * jnp.moveaxis(factor, 1, 2)[..., None] + summed
    return (peak_new, total_new, summed_new)


def body(
    latents,
    stale_kv,
    frame_ids,
    timestep,
    conv_weight,
    time_proj,
    spatial_qkv,
    spatial_out,
    temporal_qkv,
    temporal_out,
    frame_table,
):
    frames_here, rows, width, chans = latents.shape
    per_group = chans // GROUPS
    head_dim = chans // HEADS
    block = rows * width
    values = latents.astype(jnp.float32)
    grouped = values.reshape(frames_here, block, GROUPS, per_group)
    sums, squares = lax.psum(
        (jnp.sum(grouped, axis=(1, 3)), jnp.sum(grouped * grouped, axis=(1, 3))), "patch"
    )
    count = block * per_group * lax.axis_size("patch")
    mean = sums / count
    var = squares / count - mean * mean
    normed = (grouped - mean[:, None, :, None]) * lax.rsqrt(var + 1e-05)[:, None, :, None]
    act = jax.nn.silu(normed).astype(jnp.bfloat16).reshape(frames_here, rows, width, chans)
    padded = extended(act, (("patch", 1),), 1)
    padded = jnp.pad(padded, ((0, 0), (0, 0), (1, 1), (0, 0)))
    conv = jnp.zeros((frames_here, rows, width, chans), jnp.float32)
    for row_step in range(3):
        for col_step in range(3):
            window = padded[:, row_step : row_step + rows, col_step : col_step + width]
            conv = conv + jnp.einsum(
                "frwc,cd->frwd",
                window,
                conv_weight[row_step, col_step],
                preferred_element_type=jnp.float32,
            )
    half = chans // 2
    freqs = jnp.exp(-math.log(10000.0) * jnp.arange(half, dtype=jnp.float32) / half)
    angles = timestep[0].astype(jnp.float32) * freqs
    emb = jnp.concatenate([jnp.cos(angles), jnp.sin(angles)]).astype(jnp.bfloat16)
    bias = jnp.dot(emb[None], time_proj, preferred_element_type=jnp.float32)[0]
    hidden1 = (values + conv + bias).reshape(frames_here, block, chans)
    norm1 = layer_norm(hidden1).astype(jnp.bfloat16)
    projected = jnp.einsum(
        "ftc,ce->fte", norm1, spatial_qkv, preferred_element_type=jnp.float32
    ).astype(jnp.bfloat16)
    queries = projected[..., :chans].reshape(frames_here, block, HEADS, head_dim)
    fresh = projected[..., chans:]
    fresh_keys = fresh[..., :chans].reshape(frames_here, block, HEADS, head_dim)
    fresh_values = fresh[..., chans:].reshape(frames_here, block, HEADS, head_dim)
    own = lax.axis_index("patch")
    start_carry = (
        jnp.full((frames_here, HEADS, block), -1e30, jnp.float32),
        jnp.zeros((frames_here, HEADS, block), jnp.float32),
        jnp.zeros((frames_here, block, HEADS, head_dim), jnp.float32),
    )
    first = attend(start_carry, queries, fresh_keys, fresh_values, True)
    piece = lax.all_gather(stale_kv, "patch", axis=1, tiled=True)
    shards = piece.shape[1] // rows
    stacked = jnp.moveaxis(piece.reshape(frames_here, shards, block, 2 * chans), 1, 0)

    def step(state, item):
        shard_kv, offset = item
        valid = offset != own
        keys = shard_kv[..., :chans].reshape(frames_here, block, HEADS, head_dim)
        vals = shard_kv[..., chans:].reshape(frames_here, block, HEADS, head_dim)
        return (attend(state, queries, keys, vals, valid), None)

    state, unused = lax.scan(step, first, (stacked, jnp.arange(shards, dtype=jnp.int32)))
    peak, total, summed = state
    spatial = (
        (summed / jnp.moveaxis(total, 1, 2)[..., None])
        .reshape(frames_here, block, chans)
        .astype(jnp.bfloat16)
    )
    hidden2 = hidden1 + jnp.einsum(
        "ftc,cd->ftd", spatial, spatial_out, preferred_element_type=jnp.float32
    )
    hidden2 = hidden2.astype(jnp.bfloat16)
    across = lax.all_to_all(hidden2, "frame", split_axis=1, concat_axis=0, tiled=True)
    frames_all = across.shape[0]
    onehot = (
        frame_ids[:, None] == jnp.arange(frame_table.shape[0], dtype=jnp.int32)[None, :]
    ).astype(jnp.bfloat16)
    position = jnp.dot(onehot, frame_table, preferred_element_type=jnp.float32)
    base = across.astype(jnp.float32)
    norm2 = layer_norm(base + position[:, None, :]).astype(jnp.bfloat16)
    temporal_proj = jnp.einsum(
        "ftc,ce->fte", norm2, temporal_qkv, preferred_element_type=jnp.float32
    ).astype(jnp.bfloat16)
    positions = temporal_proj.shape[1]
    split_proj = temporal_proj.reshape(frames_all, positions, 3, HEADS, head_dim)
    scores = jnp.einsum(
        "ftha,gtha->thfg",
        split_proj[:, :, 0],
        split_proj[:, :, 1],
        preferred_element_type=jnp.float32,
    ) / math.sqrt(head_dim)
    peak_t = jnp.max(scores, axis=-1, keepdims=True)
    weights = jnp.exp(scores - peak_t)
    total_t = jnp.sum(weights, axis=-1)
    summed_t = jnp.einsum(
        "thfg,gtha->ftha",
        weights.astype(jnp.bfloat16),
        split_proj[:, :, 2],
        preferred_element_type=jnp.float32,
    )
    temporal = (
        (summed_t / jnp.transpose(total_t, (2, 0, 1))[..., None])
        .reshape(frames_all, positions, chans)
        .astype(jnp.bfloat16)
    )
    finished = (
        base + jnp.einsum("ftc,cd->ftd", temporal, temporal_out, preferred_element_type=jnp.float32)
    ).astype(jnp.bfloat16)
    returned = lax.all_to_all(finished, "frame", split_axis=0, concat_axis=1, tiled=True)
    result = returned.reshape(frames_here, rows, width, chans)
    return (result, fresh.reshape(frames_here, rows, width, 2 * chans))


def solution(mesh):
    return jax.shard_map(
        body,
        mesh=mesh,
        in_specs=(
            P("frame", "patch", None, None),
            P("frame", "patch", None, None),
            P(),
            P(),
            P(),
            P(),
            P(),
            P(),
            P(),
            P(),
            P(),
        ),
        out_specs=(P("frame", "patch", None, None), P("frame", "patch", None, None)),
        check_vma=False,
    )
```

profile of v0, /device:TPU:1, one launch (start us, length us, event | category | flops | bytes accessed | tf_op | source)
XLA Modules:
  0.0 396.9 jit_solution(11571974750541881714)
XLA Ops:
  9.5 54.9 %all-reduce.1 = (f32[1,32]{1,0:T(1,128)S(1)}, f32[1,32]{1,0:T(1,128)S(1)}) all-reduce(f32[1,32]{1,0:T(1,128)S(1)} %bitcast.268, f32[1,32]{1,0:T(1,128)S(1)} %bitcast.269), channel_id=1, replica_groups=mesh['frame'=32,'patch'=16] {'patch'}, use_global_device_ids=true, to_apply=%region_5.6 | all-reduce | flops 64 | bytes 512 | tf_op jit(solution)/shard_map/psum | solution.py:67
  67.3 4.0 %collective-permute-start = (bf16[1,1,128,320]{2,3,1,0:T(8,128)(2,1)S(1)}, bf16[1,1,128,320]{2,3,1,0:T(8,128)(2,1)S(1)}, u32[]{:S(2)}, u32[]{:S(2)}) collective-permute-start(bf16[1,1,128,320]{2,3,1,0:T(8,128)(2,1)S(1)} %get-tuple-element.101), channel_id=1, source_target_pairs={{0,1},{1,2},{2,3},{3,4},{4,5},{5,6},{6,7},{7,8},{8,9},{9,10},{10,1... | collective-permute-start | bytes 245768 | tf_op jit(solution)/shard_map/ppermute | solution.py:17
  82.0 117.5 %all-gather.2.cloned.1.call-done = bf16[1,48,128,640]{3,2,0,1:T(8,128)(2,1)} async-done(((bf16[1,3,128,640]{3,2,0,1:T(8,128)(2,1)}), bf16[1,48,128,640]{3,2,0,1:T(8,128)(2,1)}) %all-gather.2.cloned.1.call-update) | async-done | bytes 7864336 | tf_op jit(solution)/shard_map/all_gather | solution.py:108
  199.5 135.6 %while.14 = (s32[]{:T(128)}, f32[1,5,384]{2,1,0:T(8,128)S(1)}, f32[1,5,384]{2,1,0:T(8,128)S(1)}, f32[1,384,5,64]{1,3,2,0:T(8,128)S(1)}, s32[16]{0:T(128)S(1)}, /...) while((s32[]{:T(128)}, f32[1,5,384]{2,1,0:T(8,128)S(1)}, ...), condition=%wide.region_13.14_spmd, body=%wide.region_10.13_spmd.sunk | while | flops 196369920 | bytes 25436316 | solution.py:119
  200.9 2.3 bitcast_reduce_fusion.2
  204.6 2.6 fusion.130
  209.4 2.3 bitcast_reduce_fusion.2
  213.0 2.6 fusion.130
  217.9 2.3 bitcast_reduce_fusion.2
  221.5 2.6 fusion.130
  226.3 2.3 bitcast_reduce_fusion.2
  230.0 2.6 fusion.130
  234.8 2.3 bitcast_reduce_fusion.2
  238.5 2.6 fusion.130
  243.3 2.3 bitcast_reduce_fusion.2
  246.9 2.6 fusion.130
  255.4 2.6 fusion.130
  263.9 2.6 fusion.130
  272.3 2.6 fusion.130
  280.8 2.6 fusion.130
  289.3 2.6 fusion.130
  297.8 2.6 fusion.130
  306.2 2.6 fusion.130
  314.7 2.6 fusion.130
  323.2 2.6 fusion.130
  331.6 2.6 fusion.130
  336.7 2.5 reduce.23
  340.3 9.9 %all-to-all-start = ((bf16[32,2,1920]{2,1,0:T(2,128)(2,1)}), bf16[32,2,1920]{2,1,0:T(2,128)(2,1)S(1)}, u32[]{:S(2)}, u32[]{:S(2)}) async-start(bf16[32,2,1920]{2,1,0:T(2,128)(2,1)} %reshape.363), calls=%async_computation | async-start | bytes 491520 | tf_op jit(solution)/shard_map/all_to_all | solution.py:130
  350.6 10.6 %all-to-all-done = bf16[32,2,1920]{2,1,0:T(2,128)(2,1)S(1)} async-done(((bf16[32,2,1920]{2,1,0:T(2,128)(2,1)}), bf16[32,2,1920]{2,1,0:T(2,128)(2,1)S(1)}, u32[]{:S(2)}, u32[]{:S(2)}) %all-to-all-start) | async-done | bytes 245792 | tf_op jit(solution)/shard_map/all_to_all | solution.py:130
  364.7 2.8 reshape.345
  371.4 3.7 all-to-all-start.1
  376.1 13.0 %all-to-all-done.1 = bf16[32,12,320]{2,1,0:T(8,128)(2,1)S(1)} async-done(((bf16[32,12,320]{2,1,0:T(8,128)(2,1)}), bf16[32,12,320]{2,1,0:T(8,128)(2,1)S(1)}, u32[]{:S(2)}, u32[]{:S(2)}) %all-to-all-start.1) | async-done | bytes 245792 | tf_op jit(solution)/shard_map/all_to_all | solution.py:166
  (268 shorter events, 96.0 us)
Async XLA Ops:
  7.2 71.4 %copy-start = (bf16[320,960]{1,0:T(8,128)(2,1)S(1)}, bf16[320,960]{1,0:T(8,128)(2,1)}, u32[]{:S(2)}) copy-start(bf16[320,960]{1,0:T(8,128)(2,1)} %param.19) | copy-start | bytes 1843204
  7.2 66.4 %copy-start.5 = (bf16[3,3,320,320]{3,2,1,0:T(8,128)(2,1)S(1)}, bf16[3,3,320,320]{3,2,1,0:T(8,128)(2,1)}, u32[]{:S(2)}) copy-start(bf16[3,3,320,320]{3,2,1,0:T(8,128)(2,1)} %param.17) | copy-start | bytes 5529604
  7.2 192.3 %all-gather.2.cloned.1.call-start = ((), (), s32[]{:S(2)}) async-start(), calls=%async_computation.2 | async-start | bytes 8355840 | tf_op jit(solution)/shard_map/all_gather | solution.py:108
  66.0 7.2 %collective-permute-start.1 = (bf16[1,1,128,320]{2,3,1,0:T(8,128)(2,1)S(1)}, bf16[1,1,128,320]{2,3,1,0:T(8,128)(2,1)S(1)}, u32[]{:S(2)}, u32[]{:S(2)}) collective-permute-start(bf16[1,1,128,320]{2,3,1,0:T(8,128)(2,1)S(1)} %get-tuple-element.102), channel_id=1, source_target_pairs={{1,0},{2,1},{3,2},{4,3},{5,4},{6,5},{7,6},{8,7},{9,8},{10,9},{11,1... | collective-permute-start | bytes 245768 | tf_op jit(solution)/shard_map/ppermute | solution.py:20
  67.3 5.9 %collective-permute-start = (bf16[1,1,128,320]{2,3,1,0:T(8,128)(2,1)S(1)}, bf16[1,1,128,320]{2,3,1,0:T(8,128)(2,1)S(1)}, u32[]{:S(2)}, u32[]{:S(2)}) collective-permute-start(bf16[1,1,128,320]{2,3,1,0:T(8,128)(2,1)S(1)} %get-tuple-element.101), channel_id=1, source_target_pairs={{0,1},{1,2},{2,3},{3,4},{4,5},{5,6},{6,7},{7,8},{8,9},{9,10},{10,1... | collective-permute-start | bytes 245768 | tf_op jit(solution)/shard_map/ppermute | solution.py:17
  75.1 1.5 copy-start.6
  199.5 135.7 %copy-start.8 = (bf16[320,320]{1,0:T(8,128)(2,1)S(1)}, bf16[320,320]{1,0:T(8,128)(2,1)}, u32[]{:S(2)}) copy-start(bf16[320,320]{1,0:T(8,128)(2,1)} %param.20) | copy-start | bytes 614404
  204.5 2.7 copy-start.1
  213.0 2.7 copy-start.1
  221.5 2.7 copy-start.1
  230.0 2.7 copy-start.1
  238.4 2.7 copy-start.1
  246.9 2.7 copy-start.1
  255.4 2.7 copy-start.1
  263.8 2.7 copy-start.1
  272.3 2.7 copy-start.1
  280.8 2.7 copy-start.1
  289.3 2.7 copy-start.1
  297.7 2.7 copy-start.1
  306.2 2.7 copy-start.1
  314.7 2.7 copy-start.1
  323.1 2.7 copy-start.1
  331.6 2.7 copy-start.1
  335.1 15.2 %copy-start.10 = (bf16[64,320]{1,0:T(8,128)(2,1)S(1)}, bf16[64,320]{1,0:T(8,128)(2,1)}, u32[]{:S(2)}) copy-start(bf16[64,320]{1,0:T(8,128)(2,1)} %param.23) | copy-start | bytes 122884
  335.1 15.2 %copy-start.11 = (s32[32]{0:T(128)S(1)}, s32[32]{0:T(128)}, u32[]{:S(2)}) copy-start(s32[32]{0:T(128)} %param.15) | copy-start | bytes 388
  340.3 20.9 %all-to-all-start = ((bf16[32,2,1920]{2,1,0:T(2,128)(2,1)}), bf16[32,2,1920]{2,1,0:T(2,128)(2,1)S(1)}, u32[]{:S(2)}, u32[]{:S(2)}) async-start(bf16[32,2,1920]{2,1,0:T(2,128)(2,1)} %reshape.363), calls=%async_computation | async-start | bytes 491520 | tf_op jit(solution)/shard_map/all_to_all | solution.py:130
  361.7 1.5 copy-start.7
  362.4 0.9 copy-start.2
  368.8 1.3 copy-start.3
  368.8 1.3 copy-start.9
  369.4 5.7 %slice-start = ((bf16[1,384,960]{1,2,0:T(8,128)(2,1)}), bf16[1,384,640]{1,2,0:T(8,128)(2,1)S(1)}, s32[]{:S(2)}) async-start(bf16[1,384,960]{1,2,0:T(8,128)(2,1)} %copy-done.4), calls=%async_computation.3 | async-start | bytes 983040 | tf_op jit(solution)/shard_map/slice | solution.py:98
  371.4 17.6 %all-to-all-start.1 = ((bf16[32,12,320]{2,1,0:T(8,128)(2,1)}), bf16[32,12,320]{2,1,0:T(8,128)(2,1)S(1)}, u32[]{:S(2)}, u32[]{:S(2)}) async-start(bf16[32,12,320]{2,1,0:T(8,128)(2,1)} %copy.82), calls=%async_computation.1 | async-start | bytes 786432 | tf_op jit(solution)/shard_map/all_to_all | solution.py:166
  (1 other events, 0.9 us)
Sparse Core Ops, SparseCore 0:
  11.2 188.2 all-gather.1
where the time goes:
time: 398 us; the launch traced here: 397 us
  waiting for transfers between devices  142 us (36%)
  matrix products  58.7 us (15%)
  blocking collectives  54.9 us (14%)
  other arithmetic  48.8 us (12%)
  local copies, waits for them, and re-layouts  46.7 us (12%)
  starting transfers between devices  18.9 us (5%)
  between operations  15.2 us (4%)
  loops' own time  12 us (3%)
    all_gather x1, waiting for transfers between devices, body(): piece = lax.all_gather(stale_kv, 'patch', axis=1, tiled=True)  117 us
    psum x1, blocking collectives, body(): lax.psum((jnp.sum(grouped, axis=(1, 3)), jnp.sum(grouped * grouped, axis=...  54.9 us
    reduce_sum x17, other arithmetic, attend(): total_new = total_old * factor + jnp.sum(weights, axis=-1)  41.7 us
    dot_general x17, matrix products, attend(): jnp.einsum('fqhd,fkhd->fhqk', queries, keys, preferred_element_type=jnp.f...  37.1 us
    dynamic_slice x48, local copies, waits for them, and re-layouts, body(): lax.scan(step, first, (stacked, jnp.arange(shards, dtype=jnp.int32)))  31.9 us
    all_to_all x1, waiting for transfers between devices, body(): lax.all_to_all(finished, 'frame', split_axis=0, concat_axis=1, tiled=True)  13 us
    dot_general x17, matrix products, attend(): jnp.einsum('fhqk,fkhd->fqhd', weights.astype(jnp.bfloat16), values, prefe...  12.1 us
    another operation x1, loops' own time, body(): lax.scan(step, first, (stacked, jnp.arange(shards, dtype=jnp.int32)))  12 us
  transfers between devices with their start and end apart: 5, of which 3 were waited for; matrix products, arithmetic and copies ran while one was open for 3% of the time, Pallas kernels for 0%

commit v1 on v0

v1 whole, which is shorter than its diff:
```python
import functools
import math

import jax
import jax.numpy as jnp
from jax import lax
from jax.experimental import pallas as pl
from jax.experimental.pallas import tpu as pltpu
from jax.sharding import PartitionSpec as P

HEADS = 5
GROUPS = 32
F32 = jnp.float32
BF16 = jnp.bfloat16
MESH = pl.DeviceIdType.MESH
LOG2E = math.log2(math.e)
HIGHEST = lax.Precision.HIGHEST

STAGES = (((1, 2, True), (1, 2, False), (0, 0, False)), ((0, 1, True), (0, 1, False)))
FIRST = (0, 3)
FRESH = 8
STEPS = (
    (0, 0, FRESH, 1),
    (1, 0, FRESH, 1),
    (0, 0, 1, 2),
    (1, 0, 1, 2),
    (0, 0, 3, 2),
    (1, 0, 3, 2),
    (0, 1, 0, 1),
    (0, 1, 1, 2),
    (0, 1, 3, 2),
    (0, 1, 5, 2),
    (1, 1, 0, 1),
    (1, 1, 1, 2),
    (0, 1, 7, 1),
    (1, 1, 3, 2),
    (0, 0, 5, 2),
    (1, 1, 5, 2),
    (0, 0, 7, 1),
    (1, 1, 7, 1),
    (1, 0, 5, 2),
    (1, 0, 7, 1),
)


def iota(shape, dim):
    return lax.broadcasted_iota(jnp.int32, shape, dim)


def dot(a, b, precision=None):
    return lax.dot_general(
        a, b, (((1,), (0,)), ((), ())), preferred_element_type=F32, precision=precision
    )


def dot_nt(a, b, precision=None):
    return lax.dot_general(
        a, b, (((1,), (1,)), ((), ())), preferred_element_type=F32, precision=precision
    )


def layer_norm(values):
    centre = values - jnp.mean(values, axis=-1, keepdims=True)
    spread = jnp.mean(centre * centre, axis=-1, keepdims=True)
    return centre * lax.rsqrt(spread + 1e-05)


def group_of_channel(chans):
    per_group = chans // GROUPS
    chan = iota((chans, 128), 0)
    group = iota((chans, 128), 1)
    inside = (chan >= group * per_group) & (chan < (group + 1) * per_group)
    return jnp.where(inside, 1.0, 0.0).astype(F32)


def from_step(i, k):
    return lax.div(i - k + 32, 32)


def lookup(i, values):
    out = values[0]
    for k in range(1, len(values)):
        if values[k] != values[k - 1]:
            out = out + (values[k] - values[k - 1]) * from_step(i, k)
    return out


def kernel(
    rows,
    width,
    chans,
    lat_in,
    stale_in,
    time_ref,
    conv_in,
    tproj_in,
    qkv_in,
    wout_in,
    ids_in,
    table_in,
    tqkv_in,
    tout_in,
    res_out,
    fresh_out,
    lat_t,
    stale_v,
    conv_w,
    tproj_v,
    qkv_v,
    wout_v,
    ids_v,
    table_v,
    tqkv_v,
    tout_v,
    lat,
    kv_a,
    kv_b,
    halo,
    act,
    stat_out,
    stat_in,
    hidden1,
    wq,
    fresh_v,
    qbuf_a,
    qbuf_b,
    qmask,
    peak,
    acc,
    obuf_a,
    obuf_b,
    lse_a,
    lse_b,
    hid,
    position,
    other,
    twq,
    gathered,
    proj,
    done,
    load_sem,
    halo_send,
    halo_recv,
    stat_send,
    stat_recv,
    ring_send,
    ring_recv,
    part_send,
    part_recv,
    own_sem,
    out_send,
    out_recv,
    back_send,
    back_recv,
):
    block = rows * width
    half = block // 2
    me = lax.axis_index("patch")
    n_patch = lax.axis_size("patch")
    ring = n_patch // 2
    z = lax.rem(me, ring)
    base_z = me - z
    right = base_z + lax.rem(z + 1, ring)
    left = base_z + lax.rem(z + ring - 1, ring)
    partner = lax.rem(me + ring, n_patch)
    frame = lax.axis_index("frame")
    frames = lax.axis_size("frame")
    kv = (kv_a, kv_b)
    qbuf = (qbuf_a, qbuf_b)


    loads = [
        pltpu.make_async_copy(src, dst, load_sem.at[i])
        for i, (src, dst) in enumerate(
            (
                (stale_in, stale_v),
                (lat_in, lat_t),
                (tproj_in, tproj_v),
                (conv_in, conv_w),
                (qkv_in, qkv_v),
                (wout_in, wout_v),
                (ids_in, ids_v),
                (table_in, table_v),
                (tqkv_in, tqkv_v),
                (tout_in, tout_v),
            )
        )
    ]
    (
        load_stale,
        load_lat,
        load_tproj,
        load_conv,
        load_qkv,
        load_wout,
        load_ids,
        load_table,
        load_tqkv,
        load_tout,
    ) = loads

    def ring_copy(stage, direction, i):
        dist = i // 2 + 1
        part = i % 2 if direction == 0 else 1 - i % 2
        window = pl.ds(part * half, half)
        dst_slot = 7 if dist == 4 else 2 * dist - 1 + direction
        src_slot = 0 if dist == 1 else 2 * dist - 3 + direction
        return pltpu.make_async_remote_copy(
            src_ref=kv[stage].at[src_slot, window],
            dst_ref=kv[stage].at[dst_slot, window],
            send_sem=ring_send.at[stage, direction, i],
            recv_sem=ring_recv.at[stage, direction, i],
            device_id={"patch": right if direction == 0 else left},
            device_id_type=MESH,
        )

    def ring_start(stage):
        for i in range(2):
            for direction in range(2):
                ring_copy(stage, direction, i).start()

    def ring_wait(stage, e):
        for direction in range(2):
            ring_copy(stage, direction, e).wait_recv()

    def ring_forward(stage, e):
        for direction in range(2):
            ring_copy(stage, direction, e + 2).start()

    def ring_event(stage, e):
        for direction in range(2):
            ring_copy(stage, direction, e).wait_recv()
            if e + 2 < 7:
                ring_copy(stage, direction, e + 2).start()

    def halo_copy(direction):
        window = pl.ds((rows - 1) * width, width) if direction == 0 else pl.ds(0, width)
        return pltpu.make_async_remote_copy(
            src_ref=lat.at[window],
            dst_ref=halo.at[direction],
            send_sem=halo_send.at[direction],
            recv_sem=halo_recv.at[direction],
            device_id={"patch": me + 1 if direction == 0 else me - 1},
            device_id_type=MESH,
        )

    def stat_copy(k):
        return pltpu.make_async_remote_copy(
            src_ref=stat_out,
            dst_ref=stat_in.at[k],
            send_sem=stat_send.at[k],
            recv_sem=stat_recv.at[k],
            device_id={"patch": lax.rem(me + k, n_patch)},
            device_id_type=MESH,
        )

    def part_copy(src, dst, k):
        return pltpu.make_async_remote_copy(
            src_ref=src,
            dst_ref=dst,
            send_sem=part_send.at[k],
            recv_sem=part_recv.at[k],
            device_id={"patch": partner},
            device_id_type=MESH,
        )

    query_copies = [part_copy(qbuf[s].at[0], qbuf[s].at[1], s) for s in range(2)]
    output_copies = [(part_copy(obuf_a.at[0], obuf_a.at[1], 2), part_copy(lse_a.at[0], lse_a.at[1], 3))]
    for c in range(rows):
        window = pl.ds(c * width, width)
        output_copies.append(
            (
                part_copy(obuf_b.at[0, window], obuf_b.at[1, window], 4 + 2 * c),
                part_copy(lse_b.at[0, c], lse_b.at[1, c], 5 + 2 * c),
            )
        )

    def group_rows(g):
        return pl.ds(pl.multiple_of(g * 16, 16), 16)

    per_row = width // 16

    def is_active(f):
        return lax.rem(f, 4) < rows

    def group_of(f):
        return lax.rem(f, 4) * per_row + lax.div(f, 4)

    def out_copy(target):
        return pltpu.make_async_remote_copy(
            src_ref=hid.at[group_rows(group_of(target))],
            dst_ref=gathered.at[group_rows(frame)],
            send_sem=out_send.at[target],
            recv_sem=out_recv.at[frame],
            device_id={"frame": target},
            device_id_type=MESH,
        )

    def back_copy(target):
        return pltpu.make_async_remote_copy(
            src_ref=done.at[group_rows(target)],
            dst_ref=res_out.at[group_rows(group_of(frame))],
            send_sem=back_send.at[target],
            recv_sem=back_recv.at[frame],
            device_id={"frame": target},
            device_id_type=MESH,
        )

    def arrival(source, buffer, rows_of_it, sems):
        return pltpu.make_async_remote_copy(
            src_ref=done.at[pl.ds(0, 16)],
            dst_ref=buffer.at[rows_of_it],
            send_sem=out_send.at[0],
            recv_sem=sems.at[source],
            device_id={"frame": source},
            device_id_type=MESH,
        )


    barrier = pltpu.get_barrier_semaphore()

    def greet_patch(k, carry):
        pl.semaphore_signal(
            barrier,
            inc=1,
            device_id={"patch": lax.rem(me + k, n_patch)},
            device_id_type=MESH,
        )
        return carry

    def greet_frame(k, carry):
        pl.semaphore_signal(
            barrier,
            inc=1,
            device_id={"frame": lax.rem(frame + k, frames)},
            device_id_type=MESH,
        )
        return carry

    lax.fori_loop(1, n_patch, greet_patch, 0)
    lax.fori_loop(1, frames, greet_frame, 0)
    for load in loads:
        load.start()

    low = iota((block, 128), 1) < 64

    def arrange(source, slot):
        kv_a[slot, :, 0:128] = jnp.where(low, source[:, 256:384], source[:, 512:640])
        kv_a[slot, :, 128:256] = source[:, 0:128]
        kv_a[slot, :, 256:384] = source[:, 320:448]
        kv_b[slot, :, 0:128] = source[:, 128:256]
        kv_b[slot, :, 128:256] = source[:, 448:576]

    load_stale.wait()
    arrange(stale_v, 0)
    load_lat.wait()
    for r in range(rows):
        lat[r * width : (r + 1) * width] = lat_t[r].astype(F32).T.astype(BF16)

    pl.semaphore_wait(barrier, n_patch - 1 + frames - 1)
    ring_start(0)

    @pl.when(me < n_patch - 1)
    def _():
        halo_copy(0).start()

    @pl.when(me > 0)
    def _():
        halo_copy(1).start()

    values = lat[...].astype(F32)
    col_sum = jnp.sum(values, axis=0, keepdims=True)
    col_sq = jnp.sum(values * values, axis=0, keepdims=True)
    row8 = iota((8, chans), 0)
    cols = jnp.where(row8 == 0, col_sum, jnp.where(row8 == 1, col_sq, 0.0))
    member = group_of_channel(chans)
    stat_out[...] = dot(cols, member, HIGHEST)

    def send_stat(k, carry):
        stat_copy(k).start()
        return carry

    lax.fori_loop(1, n_patch, send_stat, 0)
    ring_start(1)

    load_tproj.wait()
    lane_c = iota((8, chans), 1)
    half_c = chans // 2
    order = jnp.where(lane_c < half_c, lane_c, lane_c - half_c).astype(F32)
    freqs = jnp.exp(-math.log(10000.0) * order / half_c)
    angles = time_ref[0].astype(F32) * freqs
    emb = jnp.where(lane_c < half_c, jnp.cos(angles), jnp.sin(angles)).astype(BF16)
    bias = dot(emb, tproj_v[...])[0:1]
    load_conv.wait()
    load_qkv.wait()
    wq[...] = jnp.zeros_like(wq)
    wq[:, 0:chans] = qkv_v[:, 0:chans]
    peak[...] = jnp.full(peak.shape, -1e30, F32)
    acc[...] = jnp.zeros(acc.shape, F32)


    def wait_stat(k, carry):
        stat_copy(k).wait_recv()
        return carry

    lax.fori_loop(1, n_patch, wait_stat, 0)
    total = stat_out[...]
    for k in range(1, 16):
        total = total + stat_in[k]
    count = block * (chans // GROUPS) * n_patch
    mean = total[0:1] / count
    var = total[1:2] / count - mean * mean
    rstd = lax.rsqrt(var + 1e-05)
    row8g = iota((8, 128), 0)
    spread = dot_nt(jnp.where(row8g == 0, mean, jnp.where(row8g == 1, rstd, 0.0)), member, HIGHEST)
    mean_c, rstd_c = spread[0:1], spread[1:2]

    def activate(x):
        normed = (x.astype(F32) - mean_c) * rstd_c
        return (normed / (1.0 + jnp.exp(-normed))).astype(BF16)

    act[width : width + block] = activate(lat[...])

    @pl.when(me > 0)
    def _():
        halo_copy(0).wait_recv()
        act[0:width] = activate(halo[0])

    @pl.when(me == 0)
    def _():
        act[0:width] = jnp.zeros((width, chans), BF16)

    @pl.when(me < n_patch - 1)
    def _():
        halo_copy(1).wait_recv()
        act[width + block :] = activate(halo[1])

    @pl.when(me == n_patch - 1)
    def _():
        act[width + block :] = jnp.zeros((width, chans), BF16)

    ring_event(0, 0)


    column = iota((block, chans), 0) & (width - 1)

    def conv_column(step):
        out = dot(act[0:block], conv_w[0, step])
        out = out + dot(act[width : width + block], conv_w[1, step])
        return out + dot(act[2 * width : 2 * width + block], conv_w[2, step])

    conv = conv_column(1)
    conv = conv + jnp.where(column == 0, 0.0, pltpu.roll(conv_column(0), 1, 0))
    ring_event(0, 1)
    conv = conv + jnp.where(column == width - 1, 0.0, pltpu.roll(conv_column(2), block - 1, 0))
    h1 = lat[...].astype(F32) + conv + bias
    hidden1[...] = h1
    norm1 = layer_norm(h1).astype(BF16)
    queries = dot(norm1, wq[...]) * (LOG2E / 8.0)
    low_half = iota((half, 128), 1) < 64
    qbuf_a[0, 0:block] = queries[:, 0:128].astype(BF16)
    folded = jnp.where(
        low_half, queries[0:half, 256:384], pltpu.roll(queries[half:, 256:384], 64, 1)
    )
    qbuf_a[0, block:] = folded.astype(BF16)
    query_copies[0].start()
    qbuf_b[0] = queries[:, 128:256].astype(BF16)
    query_copies[1].start()
    ring_event(1, 0)
    ring_event(1, 1)
    fresh_v[...] = dot(norm1, qkv_v[:, chans:]).astype(BF16)
    store_fresh = pltpu.make_async_copy(fresh_v, fresh_out, own_sem.at[2])
    store_fresh.start()
    arrange(fresh_v, FRESH)

    def mask_queries(stage, which):
        def keep(tile, lanes):
            return jnp.where(lanes, tile, jnp.zeros_like(tile))

        if stage == 0:
            tile = qbuf_a[which, 0:block]
            qmask[which, 0] = keep(tile, low)
            qmask[which, 1] = keep(tile, ~low)
            tile = qbuf_a[which, block:].astype(F32)
            qmask[which, 2, 0:half] = jnp.where(low_half, tile, 0.0).astype(BF16)
            tile = pltpu.roll(tile, 64, 1)
            qmask[which, 2, half:] = jnp.where(low_half, tile, 0.0).astype(BF16)
        else:
            tile = qbuf_b[which]
            qmask[which, 3] = keep(tile, low)
            qmask[which, 4] = keep(tile, ~low)

    mask_queries(0, 0)
    mask_queries(1, 0)


    def attend(stage, which, slot, slots):
        heads = STAGES[stage]
        keys = slots * block
        low_keys = iota((keys, 128), 1) < 64

        def tile_of(t):
            return kv[stage][pl.ds(slot, slots), :, t * 128 : t * 128 + 128].reshape(keys, 128)

        def scores_of(j):
            return dot_nt(qmask[which, FIRST[stage] + j], tile_of(heads[j][0]))

        accs = [acc[which, FIRST[stage] + j] for j in range(len(heads))]
        peaks = [peak[which, FIRST[stage] + j] for j in range(len(heads))]
        scores = scores_of(0)
        results = []
        for j, (_, vt, in_low) in enumerate(heads):
            following = scores_of(j + 1) if j + 1 < len(heads) else None
            top = jnp.maximum(peaks[j], jnp.max(scores, axis=1, keepdims=True))
            weights = jnp.exp2(scores - jnp.concatenate([top] * (keys // 128), axis=1))
            vals = tile_of(vt)
            vals = jnp.where(low_keys if in_low else ~low_keys, vals, jnp.ones_like(vals))
            scale = jnp.exp2(peaks[j] - top)
            results.append((accs[j] * scale + dot(weights.astype(BF16), vals), top))
            scores = following
        for j, (new_acc, top) in enumerate(results):
            acc[which, FIRST[stage] + j] = new_acc
            peak[which, FIRST[stage] + j] = top

    lane = iota((block, 128), 1)

    def settle(which, stage, j, window):
        a = acc[which, FIRST[stage] + j, window]
        turned = pltpu.roll(a, 64, 1)
        mine = (iota(a.shape, 1) >= 64) if STAGES[stage][j][2] else (iota(a.shape, 1) < 64)
        sums = jnp.where(mine, a, turned)
        return a / sums, peak[which, FIRST[stage] + j, window] + jnp.log2(sums)

    def part_of(c):
        if c is None:
            return 0, slice(0, block), output_copies[0]
        return 1, slice(c * width, (c + 1) * width), output_copies[1 + c]

    def finish_partner(c=None):
        stage, window, copies = part_of(c)
        outs = [settle(1, stage, j, window) for j in range(len(STAGES[stage]))]
        count_rows = window.stop - window.start
        low_rows = iota((count_rows, 128), 1) < 64
        pair = jnp.where(low_rows, outs[0][0], outs[1][0]).astype(BF16)
        if stage == 0:
            obuf_a[0, 0:block] = pair
            out = outs[2][0]
            folded = jnp.where(low_half, pltpu.roll(out[half:], 64, 1), out[0:half])
            obuf_a[0, block:] = folded.astype(BF16)
        else:
            obuf_b[0, window] = pair
        copies[0].start()
        lane = iota((count_rows, 128), 1)
        sums = jnp.zeros((count_rows, 128), F32)
        for j, (_, lse) in enumerate(outs):
            sums = jnp.where(lane == j, lse, sums)
        if stage == 0:
            lse_a[0] = sums.T[0:8]
        else:
            lse_b[0, c] = sums.T[0:8]
        copies[1].start()

    def joined(c=None):
        stage, window, copies = part_of(c)
        own = [settle(0, stage, j, window) for j in range(len(STAGES[stage]))]
        for copy in copies:
            copy.wait_recv()
        sent = lse_a[1] if stage == 0 else lse_b[1, c]
        there = jnp.concatenate([sent, jnp.zeros((120, sent.shape[1]), F32)], axis=0).T
        outs = []
        for j, (out, lse) in enumerate(own):
            if stage == 1:
                out_there = obuf_b[1, window].astype(F32)
            elif j < 2:
                out_there = obuf_a[1, 0:block].astype(F32)
            else:
                folded = obuf_a[1, block:].astype(F32)
                out_there = jnp.concatenate([folded, pltpu.roll(folded, 64, 1)], axis=0)
            lse_there = there[:, j : j + 1]
            top = jnp.maximum(lse, lse_there)
            weight = jnp.exp2(lse - top)
            weight_there = jnp.exp2(lse_there - top)
            mixed = out * weight + out_there * weight_there
            outs.append(mixed / (weight + weight_there))
        return outs

    before = {
        1: lambda: ring_event(0, 2),
        4: lambda: ring_event(0, 3),
        5: lambda: (ring_wait(1, 2), ring_wait(1, 3)),
        6: lambda: (
            ring_event(0, 4),
            ring_forward(1, 2),
            ring_forward(1, 3),
            query_copies[0].wait_recv(),
            mask_queries(0, 1),
        ),
        9: lambda: ring_event(0, 5),
        10: lambda: (query_copies[1].wait_recv(), mask_queries(1, 1)),
        12: lambda: ring_event(0, 6),
        13: lambda: (finish_partner(), ring_event(1, 4)),
        15: lambda: ring_event(1, 5),
        17: lambda: ring_event(1, 6),
        18: lambda: [finish_partner(c) for c in range(rows)],
    }

    def step(i, carry):
        for k, actions in before.items():

            @pl.when(i == k)
            def _():
                actions()

        which = lookup(i, [s[1] for s in STEPS])
        slot = lookup(i, [s[2] for s in STEPS])
        kind = lookup(i, [2 * s[0] + s[3] - 1 for s in STEPS])
        for stage in range(2):
            for slots in (1, 2):
                pl.when(kind == 2 * stage + slots - 1)(
                    functools.partial(attend, stage, which, slot, slots)
                )
        return carry

    lax.fori_loop(0, len(STEPS), step, 0)


    load_ids.wait()
    load_table.wait()
    load_tqkv.wait()
    npos = table_v.shape[0]
    everything = frames * 16
    picked = jnp.where(iota((npos, frames), 0) == ids_v[...], 1.0, 0.0).astype(BF16)
    repeat = jnp.where(
        (iota((everything, frames), 0) >> 4) == iota((everything, frames), 1), 1.0, 0.0
    ).astype(BF16)
    onehot = dot_nt(repeat, picked).astype(BF16)
    position[...] = dot(onehot, table_v[...])
    other[...] = jnp.where(
        (iota((everything, everything), 0) & 15) == (iota((everything, everything), 1) & 15),
        0.0,
        -1e30,
    )
    twq[...] = jnp.zeros_like(twq)
    for part in range(3):
        twq[:, part * 384 : part * 384 + chans] = tqkv_v[:, part * chans : (part + 1) * chans]
    load_wout.wait()
    load_tout.wait()

    def wait_stat_send(k, carry):
        stat_copy(k).wait_send()
        return carry

    lax.fori_loop(1, n_patch, wait_stat_send, 0)

    @pl.when(me < n_patch - 1)
    def _():
        halo_copy(0).wait_send()

    @pl.when(me > 0)
    def _():
        halo_copy(1).wait_send()

    for stage in range(2):
        for i in range(7):
            for direction in range(2):
                ring_copy(stage, direction, i).wait_send()
        query_copies[stage].wait_send()
    store_fresh.wait()


    first = joined()
    pair = jnp.where(low, first[0], first[1]).astype(BF16)
    last = pltpu.roll(first[2], 64, 1)[:, 0:64].astype(BF16)
    hidden1[...] = (
        hidden1[...] + dot(pair, wout_v[0:128]) + dot(last, wout_v[256:chans])
    )
    quarter = frames // 4
    low_row = iota((width, 128), 1) < 64
    for c in range(rows):
        second = joined(c)
        window = slice(c * width, (c + 1) * width)
        pair = jnp.where(low_row, second[0], second[1]).astype(BF16)
        hid[window] = (hidden1[window] + dot(pair, wout_v[128:256])).astype(BF16)

        def send_out(k, carry, c=c):
            target = lax.rem(lax.div(frame, 4) + k, quarter) * 4 + c

            @pl.when(target != frame)
            def _():
                out_copy(target).start()

            return carry

        lax.fori_loop(0, quarter, send_out, 0)


    @pl.when(is_active(frame))
    def _():
        mine = group_rows(group_of(frame))
        keep = pltpu.make_async_copy(hid.at[mine], gathered.at[group_rows(frame)], own_sem.at[0])
        keep.start()
        keep.wait()

        def wait_out(k, carry):
            source = lax.rem(frame + k, frames)
            arrival(source, gathered, group_rows(source), out_recv).wait_recv()
            return carry

        lax.fori_loop(1, frames, wait_out, 0)

        inputs = gathered[...].astype(F32)
        norm2 = layer_norm(inputs + position[...]).astype(BF16)
        proj[:, 0:384] = (dot(norm2, twq[:, 0:384]) * (LOG2E / 8.0)).astype(BF16)
        proj[:, 384:] = dot(norm2, twq[:, 384:]).astype(BF16)

        low_t = iota((everything, 128), 1) < 64

        def lanes_of(h):
            return low_t if h % 2 == 0 else ~low_t

        def scores_t(h):
            tile = (h // 2) * 128
            q = proj[:, tile : tile + 128]
            q = jnp.where(lanes_of(h), q, jnp.zeros_like(q))
            return dot_nt(q, proj[:, 384 + tile : 384 + tile + 128])

        outs = []
        scores = scores_t(0)
        for h in range(HEADS):
            following = scores_t(h + 1) if h + 1 < HEADS else None
            tile = (h // 2) * 128
            v = proj[:, 768 + tile : 768 + tile + 128]
            v = jnp.where(lanes_of(h), v, jnp.ones_like(v))
            scores = scores + other[...]
            weights = jnp.exp2(scores - jnp.max(scores, axis=1, keepdims=True)).astype(BF16)
            mixed = dot(weights, v)
            outs.append(mixed / pltpu.roll(mixed, 64, 1))
            scores = following
        temporal = jnp.concatenate(
            [
                jnp.where(low_t, outs[0], outs[1]).astype(BF16),
                jnp.where(low_t, outs[2], outs[3]).astype(BF16),
                outs[4][:, 0:64].astype(BF16),
            ],
            axis=1,
        )
        done[...] = (inputs + dot(temporal, tout_v[...])).astype(BF16)

        def send_back(k, carry):
            back_copy(lax.rem(frame + k, frames)).start()
            return carry

        lax.fori_loop(1, frames, send_back, 0)
        put = pltpu.make_async_copy(done.at[group_rows(frame)], res_out.at[mine], own_sem.at[1])
        put.start()
        put.wait()

    for copies in output_copies:
        for copy in copies:
            copy.wait_send()

    def wait_out_send(k, carry):
        target = lax.rem(frame + k, frames)

        @pl.when(is_active(target))
        def _():
            out_copy(target).wait_send()

        return carry

    lax.fori_loop(1, frames, wait_out_send, 0)

    def wait_back(k, carry):
        source = lax.rem(frame + k, frames)

        @pl.when(is_active(source))
        def _():
            arrival(source, res_out, group_rows(group_of(source)), back_recv).wait_recv()

        return carry

    lax.fori_loop(1, frames, wait_back, 0)
    @pl.when(is_active(frame))
    def _():
        def wait_back_send(k, carry):
            back_copy(lax.rem(frame + k, frames)).wait_send()
            return carry

        lax.fori_loop(1, frames, wait_back_send, 0)


def emit_kernel(res_in, fresh_in, res_out, fresh_out, res_v, res_t, fresh_v, sems):
    rows, _, width = res_out.shape
    parts = [pl.ds(width * i, width) for i in range(rows)]

    def copies(k, src, dst):
        return pltpu.make_async_copy(src, dst, sems.at[k])

    res_loads = [copies(i, res_in.at[p], res_v.at[p]) for i, p in enumerate(parts)]
    fresh_loads = [copies(3 + i, fresh_in.at[p], fresh_v.at[p]) for i, p in enumerate(parts)]
    res_stores = [copies(6 + i, res_t.at[i], res_out.at[i]) for i in range(rows)]
    fresh_stores = [copies(9 + i, fresh_v.at[p], fresh_out.at[p]) for i, p in enumerate(parts)]
    for copy in res_loads + fresh_loads:
        copy.start()
    for i in range(rows):
        res_loads[i].wait()
        res_t[i] = res_v[parts[i]].astype(F32).T.astype(BF16)
        res_stores[i].start()
    for i in range(rows):
        fresh_loads[i].wait()
        fresh_stores[i].start()
    for copy in res_stores + fresh_stores:
        copy.wait()


def body(
    latents,
    stale_kv,
    frame_ids,
    timestep,
    conv_weight,
    time_proj,
    spatial_qkv,
    spatial_out,
    temporal_qkv,
    temporal_out,
    frame_table,
):
    rows, width, chans = latents.shape[1:]
    block = rows * width
    frames = frame_ids.shape[0]
    npos = frame_table.shape[0]
    dma = pltpu.SemaphoreType.DMA
    vmem = pltpu.VMEM
    anywhere = pl.BlockSpec(memory_space=pl.ANY)
    result, fresh = pl.pallas_call(
        functools.partial(kernel, rows, width, chans),
        out_shape=(
            jax.ShapeDtypeStruct((block, chans), BF16),
            jax.ShapeDtypeStruct((block, 2 * chans), BF16),
        ),
        in_specs=[anywhere, anywhere, pl.BlockSpec(memory_space=pltpu.SMEM)] + [anywhere] * 8,
        out_specs=(anywhere, anywhere),
        scratch_shapes=[
            vmem((rows, chans, width), BF16),
            vmem((block, 2 * chans), BF16),
            vmem((3, 3, chans, chans), BF16),
            vmem((chans, chans), BF16),
            vmem((chans, 3 * chans), BF16),
            vmem((chans, chans), BF16),
            vmem((1, frames), jnp.int32),
            vmem((npos, chans), BF16),
            vmem((chans, 3 * chans), BF16),
            vmem((chans, chans), BF16),
            vmem((block, chans), BF16),
            vmem((9, block, 384), BF16),
            vmem((9, block, 256), BF16),
            vmem((2, width, chans), BF16),
            vmem((block + 2 * width, chans), BF16),
            vmem((8, 128), F32),
            vmem((16, 8, 128), F32),
            vmem((block, chans), F32),
            vmem((chans, 384), BF16),
            vmem((block, 2 * chans), BF16),
            vmem((2, block + block // 2, 128), BF16),
            vmem((2, block, 128), BF16),
            vmem((2, HEADS, block, 128), BF16),
            vmem((2, HEADS, block, 128), F32),
            vmem((2, HEADS, block, 128), F32),
            vmem((2, block + block // 2, 128), BF16),
            vmem((2, block, 128), BF16),
            vmem((2, 8, block), F32),
            vmem((2, rows, 8, width), F32),
            vmem((block, chans), BF16),
            vmem((frames * 16, chans), F32),
            vmem((frames * 16, frames * 16), F32),
            vmem((chans, 3 * 384), BF16),
            vmem((frames * 16, chans), BF16),
            vmem((frames * 16, 3 * 384), BF16),
            vmem((frames * 16, chans), BF16),
            dma((10,)),
            dma((2,)),
            dma((2,)),
            dma((16,)),
            dma((16,)),
            dma((2, 2, 7)),
            dma((2, 2, 7)),
            dma((4 + 2 * rows,)),
            dma((4 + 2 * rows,)),
            dma((4,)),
            dma((frames,)),
            dma((frames,)),
            dma((frames,)),
            dma((frames,)),
        ],
        compiler_params=pltpu.CompilerParams(
            collective_id=0, has_side_effects=True, vmem_limit_bytes=60 * 1024 * 1024
        ),
        name="layer",
    )(
        jnp.transpose(latents, (0, 1, 3, 2)).reshape(rows, chans, width),
        stale_kv.reshape(block, 2 * chans),
        timestep,
        conv_weight,
        time_proj,
        spatial_qkv,
        spatial_out,
        frame_ids.reshape(1, frames),
        frame_table,
        temporal_qkv,
        temporal_out,
    )
    result, fresh = pl.pallas_call(
        emit_kernel,
        out_shape=(
            jax.ShapeDtypeStruct((rows, chans, width), BF16),
            jax.ShapeDtypeStruct(fresh.shape, BF16),
        ),
        in_specs=[anywhere] * 2,
        out_specs=(anywhere, anywhere),
        scratch_shapes=[
            vmem(result.shape, BF16),
            vmem((rows, chans, width), BF16),
            vmem(fresh.shape, BF16),
            dma((12,)),
        ],
        compiler_params=pltpu.CompilerParams(vmem_limit_bytes=62 * 1024 * 1024),
        name="emit",
    )(result, fresh)
    result = jnp.transpose(result.reshape(1, rows, chans, width), (0, 1, 3, 2))
    return result, fresh.reshape(stale_kv.shape)


def solution(mesh):
    return jax.shard_map(
        body,
        mesh=mesh,
        in_specs=(
            P("frame", "patch", None, None),
            P("frame", "patch", None, None),
            P(),
            P(),
            P(),
            P(),
            P(),
            P(),
            P(),
            P(),
            P(),
        ),
        out_specs=(P("frame", "patch", None, None), P("frame", "patch", None, None)),
        check_vma=False,
    )
```

time: 398 us -> 95.4 us (0.24)
  waiting for transfers between devices: 142 us -> 0 us
  Pallas kernels: 0 us -> 93.8 us
  matrix products: 58.7 us -> 0 us
  blocking collectives: 54.9 us -> 0 us
  other arithmetic: 48.8 us -> 0 us
  local copies, waits for them, and re-layouts: 46.7 us -> 0 us
  starting transfers between devices: 18.9 us -> 0 us
  between operations: 15.2 us -> 1.45 us
  loops' own time: 12 us -> 0 us
    all_gather x1 -> x0, waiting for transfers between devices: 117 us -> none  [body(): piece = lax.all_gather(stale_kv, 'patch', axis=1, tiled=True)]
    pallas_call x0 -> x2, Pallas kernels: none -> 93.8 us  [the longest x1 91.7 us: body(): pl.pallas_call(functools.partial(kernel, rows, width, chans), out_shape=(...]
    dot_general x51 -> x0, matrix products: 58.7 us -> none  [the longest x17 37.1 us: attend(): jnp.einsum('fqhd,fkhd->fhqk', queries, keys, preferred_element_type=jnp.f...]
    psum x1 -> x0, blocking collectives: 54.9 us -> none  [body(): lax.psum((jnp.sum(grouped, axis=(1, 3)), jnp.sum(grouped * grouped, axis=...]
    reduce_sum x24 -> x0, other arithmetic: 43.8 us -> none  [the longest x17 41.7 us: attend(): total_new = total_old * factor + jnp.sum(weights, axis=-1)]
    dynamic_slice x48 -> x0, local copies, waits for them, and re-layouts: 31.9 us -> none  [body(): lax.scan(step, first, (stacked, jnp.arange(shards, dtype=jnp.int32)))]
    all_to_all x2 -> x0, waiting for transfers between devices: 23.6 us -> none  [the longest x1 13 us: body(): lax.all_to_all(finished, 'frame', split_axis=0, concat_axis=1, tiled=True)]
    all_to_all x2 -> x0, starting transfers between devices: 13.6 us -> none  [the longest x1 9.94 us: body(): lax.all_to_all(hidden2, 'frame', split_axis=1, concat_axis=0, tiled=True)]
  transfers between devices with their start and end apart: 5 -> 0, of which waited for: 3 -> 0; matrix products, arithmetic and copies ran while one was open for 3% -> 0% of each run, Pallas kernels for 0% -> 0%
where the time goes in v1:
time: 95.4 us; the launch traced here: 95.3 us
  Pallas kernels  93.8 us (98%)
  between operations  1.45 us (2%)
    pallas_call x1, Pallas kernels, body(): pl.pallas_call(functools.partial(kernel, rows, width, chans), out_shape=(...  91.7 us
    pallas_call x1, Pallas kernels, body(): pl.pallas_call(emit_kernel, out_shape=(jax.ShapeDtypeStruct((rows, chans,...  2.12 us

profile of v1, /device:TPU:1, one launch (start us, length us, event | category | flops | bytes accessed | tf_op | source)
XLA Modules:
  0.0 95.3 jit_solution(4915635926866206593)
XLA Ops:
  1.3 91.7 %layer.1 = (bf16[384,320]{1,0:T(8,128)(2,1)}, bf16[384,640]{1,0:T(8,128)(2,1)}) custom-call(bf16[3,320,128]{2,1,0:T(8,128)(2,1)} %bitcast.10, bf16[384,640]{1,0:T(8,128)(2,1)} %bitcast.9, s32[1]{0:T(128)S(6)} %copy.13.time_ref, bf16[3,3,320,320]{3,2,1,0:T(8,128)(2,1)} %conv_in.1, bf16[320,320]{1,0:T(8,128)(2,1)} %tproj_in.1, bf16[320,960]{1,0:T(8,128)(2,1)} %qkv_in.1, ...), custom_call_target="tpu_custom_call" | custom-call | tf_op jit(solution)/shard_map/layer/pallas_call | solution.py:836
  93.0 2.1 %emit.1 = (bf16[3,320,128]{2,1,0:T(8,128)(2,1)}, bf16[384,640]{1,0:T(8,128)(2,1)}) custom-call(bf16[384,320]{1,0:T(8,128)(2,1)} %get-tuple-element.6.res_in, bf16[384,640]{1,0:T(8,128)(2,1)} %get-tuple-element.7.fresh_in), custom_call_target="tpu_custom_call" | custom-call | tf_op jit(solution)/shard_map/emit/pallas_call | solution.py:913

commit v2 on v1

--- a/solution.py
+++ b/solution.py
@@ -234,9 +234,8 @@
                 ring_copy(stage, direction, e + 2).start()
 
     def halo_copy(direction):
-        window = pl.ds((rows - 1) * width, width) if direction == 0 else pl.ds(0, width)
         return pltpu.make_async_remote_copy(
-            src_ref=lat.at[window],
+            src_ref=lat_t.at[rows - 1 if direction == 0 else 0],
             dst_ref=halo.at[direction],
             send_sem=halo_send.at[direction],
             recv_sem=halo_recv.at[direction],
@@ -358,8 +357,6 @@
         lat[r * width : (r + 1) * width] = lat_t[r].astype(F32).T.astype(BF16)
 
     pl.semaphore_wait(barrier, n_patch - 1 + frames - 1)
-    ring_start(0)
-
     @pl.when(me < n_patch - 1)
     def _():
         halo_copy(0).start()
@@ -367,6 +364,8 @@
     @pl.when(me > 0)
     def _():
         halo_copy(1).start()
+
+    ring_start(0)
 
     values = lat[...].astype(F32)
     col_sum = jnp.sum(values, axis=0, keepdims=True)
@@ -424,7 +423,7 @@
     @pl.when(me > 0)
     def _():
         halo_copy(0).wait_recv()
-        act[0:width] = activate(halo[0])
+        act[0:width] = activate(halo[0].astype(F32).T)
 
     @pl.when(me == 0)
     def _():
@@ -433,7 +432,7 @@
     @pl.when(me < n_patch - 1)
     def _():
         halo_copy(1).wait_recv()
-        act[width + block :] = activate(halo[1])
+        act[width + block :] = activate(halo[1].astype(F32).T)
 
     @pl.when(me == n_patch - 1)
     def _():
@@ -584,11 +583,34 @@
             outs.append(mixed / (weight + weight_there))
         return outs
 
+    everything = frames * 16
+
+    def prepare_temporal():
+        load_ids.wait()
+        load_table.wait()
+        load_tqkv.wait()
+        npos = table_v.shape[0]
+        picked = jnp.where(iota((npos, frames), 0) == ids_v[...], 1.0, 0.0).astype(BF16)
+        repeat = jnp.where(
+            (iota((everything, frames), 0) >> 4) == iota((everything, frames), 1), 1.0, 0.0
+        ).astype(BF16)
+        onehot = dot_nt(repeat, picked).astype(BF16)
+        position[...] = dot(onehot, table_v[...])
+        other[...] = jnp.where(
+            (iota((everything, everything), 0) & 15) == (iota((everything, everything), 1) & 15),
+            0.0,
+            -1e30,
+        )
+        twq[...] = jnp.zeros_like(twq)
+        for part in range(3):
+            twq[:, part * 384 : part * 384 + chans] = tqkv_v[:, part * chans : (part + 1) * chans]
+
     before = {
         1: lambda: ring_event(0, 2),
         4: lambda: ring_event(0, 3),
         5: lambda: (ring_wait(1, 2), ring_wait(1, 3)),
         6: lambda: (
+            prepare_temporal(),
             ring_event(0, 4),
             ring_forward(1, 2),
             ring_forward(1, 3),
@@ -623,26 +645,6 @@
 
     lax.fori_loop(0, len(STEPS), step, 0)
 
-
-    load_ids.wait()
-    load_table.wait()
-    load_tqkv.wait()
-    npos = table_v.shape[0]
-    everything = frames * 16
-    picked = jnp.where(iota((npos, frames), 0) == ids_v[...], 1.0, 0.0).astype(BF16)
-    repeat = jnp.where(
-        (iota((everything, frames), 0) >> 4) == iota((everything, frames), 1), 1.0, 0.0
-    ).astype(BF16)
-    onehot = dot_nt(repeat, picked).astype(BF16)
-    position[...] = dot(onehot, table_v[...])
-    other[...] = jnp.where(
-        (iota((everything, everything), 0) & 15) == (iota((everything, everything), 1) & 15),
-        0.0,
-        -1e30,
-    )
-    twq[...] = jnp.zeros_like(twq)
-    for part in range(3):
-        twq[:, part * 384 : part * 384 + chans] = tqkv_v[:, part * chans : (part + 1) * chans]
     load_wout.wait()
     load_tout.wait()
 
@@ -714,43 +716,57 @@
         proj[:, 384:] = dot(norm2, twq[:, 384:]).astype(BF16)
 
         low_t = iota((everything, 128), 1) < 64
+        upper = everything // 2
 
         def lanes_of(h):
             return low_t if h % 2 == 0 else ~low_t
 
-        def scores_t(h):
-            tile = (h // 2) * 128
-            q = proj[:, tile : tile + 128]
-            q = jnp.where(lanes_of(h), q, jnp.zeros_like(q))
-            return dot_nt(q, proj[:, 384 + tile : 384 + tile + 128])
-
-        outs = []
-        scores = scores_t(0)
-        for h in range(HEADS):
-            following = scores_t(h + 1) if h + 1 < HEADS else None
-            tile = (h // 2) * 128
-            v = proj[:, 768 + tile : 768 + tile + 128]
-            v = jnp.where(lanes_of(h), v, jnp.ones_like(v))
-            scores = scores + other[...]
-            weights = jnp.exp2(scores - jnp.max(scores, axis=1, keepdims=True)).astype(BF16)
-            mixed = dot(weights, v)
-            outs.append(mixed / pltpu.roll(mixed, 64, 1))
-            scores = following
-        temporal = jnp.concatenate(
-            [
-                jnp.where(low_t, outs[0], outs[1]).astype(BF16),
-                jnp.where(low_t, outs[2], outs[3]).astype(BF16),
-                outs[4][:, 0:64].astype(BF16),
-            ],
-            axis=1,
-        )
-        done[...] = (inputs + dot(temporal, tout_v[...])).astype(BF16)
-
-        def send_back(k, carry):
-            back_copy(lax.rem(frame + k, frames)).start()
-            return carry
-
-        lax.fori_loop(1, frames, send_back, 0)
+        def masked(h, rows_of_it, first_lane, fill):
+            tile = proj[rows_of_it, first_lane + (h // 2) * 128 : first_lane + (h // 2) * 128 + 128]
+            return jnp.where(lanes_of(h)[0 : tile.shape[0]], tile, fill(tile))
+
+        def send_half(part):
+            window = slice(part * upper, (part + 1) * upper)
+
+            def scores_t(h):
+                keys = proj[:, 384 + (h // 2) * 128 : 384 + (h // 2) * 128 + 128]
+                return dot_nt(masked(h, window, 0, jnp.zeros_like), keys)
+
+            low_h = low_t[0:upper]
+            outs = []
+            scores = scores_t(0)
+            for h in range(HEADS):
+                following = scores_t(h + 1) if h + 1 < HEADS else None
+                scores = scores + other[window]
+                weights = jnp.exp2(scores - jnp.max(scores, axis=1, keepdims=True)).astype(BF16)
+                mixed = dot(weights, masked(h, slice(0, everything), 768, jnp.ones_like))
+                outs.append(mixed / pltpu.roll(mixed, 64, 1))
+                scores = following
+            temporal = jnp.concatenate(
+                [
+                    jnp.where(low_h, outs[0], outs[1]).astype(BF16),
+                    jnp.where(low_h, outs[2], outs[3]).astype(BF16),
+                    outs[4][:, 0:64].astype(BF16),
+                ],
+                axis=1,
+            )
+            done[window] = (
+                gathered[window].astype(F32) + dot(temporal, tout_v[...])
+            ).astype(BF16)
+
+            def send_back(k, carry):
+                target = part * (frames // 2) + lax.rem(frame + k, frames // 2)
+
+                @pl.when(target != frame)
+                def _():
+                    back_copy(target).start()
+
+                return carry
+
+            lax.fori_loop(0, frames // 2, send_back, 0)
+
+        send_half(0)
+        send_half(1)
         put = pltpu.make_async_copy(done.at[group_rows(frame)], res_out.at[mine], own_sem.at[1])
         put.start()
         put.wait()
@@ -855,7 +871,7 @@
             vmem((block, chans), BF16),
             vmem((9, block, 384), BF16),
             vmem((9, block, 256), BF16),
-            vmem((2, width, chans), BF16),
+            vmem((2, chans, width), BF16),
             vmem((block + 2 * width, chans), BF16),
             vmem((8, 128), F32),
             vmem((16, 8, 128), F32),

time: 95.4 us -> 93.2 us (0.977)
  Pallas kernels: 93.8 us -> 91.5 us
    pallas_call x1, Pallas kernels: 91.7 us -> 89.4 us  [body(): pl.pallas_call(functools.partial(kernel, rows, width, chans), out_shape=(...]
where the time goes in v2:
time: 93.2 us; the launch traced here: 93 us
  Pallas kernels  91.5 us (98%)
  between operations  1.45 us (2%)
    pallas_call x1, Pallas kernels, body(): pl.pallas_call(functools.partial(kernel, rows, width, chans), out_shape=(...  89.4 us
    pallas_call x1, Pallas kernels, body(): pl.pallas_call(emit_kernel, out_shape=(jax.ShapeDtypeStruct((rows, chans,...  2.12 us

profile of v2, /device:TPU:1, one launch (start us, length us, event | category | flops | bytes accessed | tf_op | source)
XLA Modules:
  0.0 93.0 jit_solution(16671491413934835346)
XLA Ops:
  1.3 89.4 %layer.1 = (bf16[384,320]{1,0:T(8,128)(2,1)}, bf16[384,640]{1,0:T(8,128)(2,1)}) custom-call(bf16[3,320,128]{2,1,0:T(8,128)(2,1)} %bitcast.10, bf16[384,640]{1,0:T(8,128)(2,1)} %bitcast.9, s32[1]{0:T(128)S(6)} %copy.13.time_ref, bf16[3,3,320,320]{3,2,1,0:T(8,128)(2,1)} %conv_in.1, bf16[320,320]{1,0:T(8,128)(2,1)} %tproj_in.1, bf16[320,960]{1,0:T(8,128)(2,1)} %qkv_in.1, ...), custom_call_target="tpu_custom_call" | custom-call | tf_op jit(solution)/shard_map/layer/pallas_call | solution.py:852
  90.7 2.1 %emit.1 = (bf16[3,320,128]{2,1,0:T(8,128)(2,1)}, bf16[384,640]{1,0:T(8,128)(2,1)}) custom-call(bf16[384,320]{1,0:T(8,128)(2,1)} %get-tuple-element.6.res_in, bf16[384,640]{1,0:T(8,128)(2,1)} %get-tuple-element.7.fresh_in), custom_call_target="tpu_custom_call" | custom-call | tf_op jit(solution)/shard_map/emit/pallas_call | solution.py:929

commit v3 on v2

--- a/solution.py
+++ b/solution.py
@@ -559,9 +559,12 @@
             lse_b[0, c] = sums.T[0:8]
         copies[1].start()
 
-    def joined(c=None):
+    def own_part(c=None):
+        stage, window, _ = part_of(c)
+        return [settle(0, stage, j, window) for j in range(len(STAGES[stage]))]
+
+    def joined(own, c=None):
         stage, window, copies = part_of(c)
-        own = [settle(0, stage, j, window) for j in range(len(STAGES[stage]))]
         for copy in copies:
             copy.wait_recv()
         sent = lse_a[1] if stage == 0 else lse_b[1, c]
@@ -648,29 +651,8 @@
     load_wout.wait()
     load_tout.wait()
 
-    def wait_stat_send(k, carry):
-        stat_copy(k).wait_send()
-        return carry
-
-    lax.fori_loop(1, n_patch, wait_stat_send, 0)
-
-    @pl.when(me < n_patch - 1)
-    def _():
-        halo_copy(0).wait_send()
-
-    @pl.when(me > 0)
-    def _():
-        halo_copy(1).wait_send()
-
-    for stage in range(2):
-        for i in range(7):
-            for direction in range(2):
-                ring_copy(stage, direction, i).wait_send()
-        query_copies[stage].wait_send()
-    store_fresh.wait()
-
-
-    first = joined()
+
+    first = joined(own_part())
     pair = jnp.where(low, first[0], first[1]).astype(BF16)
     last = pltpu.roll(first[2], 64, 1)[:, 0:64].astype(BF16)
     hidden1[...] = (
@@ -678,8 +660,9 @@
     )
     quarter = frames // 4
     low_row = iota((width, 128), 1) < 64
+    own_rows = [own_part(c) for c in range(rows)]
     for c in range(rows):
-        second = joined(c)
+        second = joined(own_rows[c], c)
         window = slice(c * width, (c + 1) * width)
         pair = jnp.where(low_row, second[0], second[1]).astype(BF16)
         hid[window] = (hidden1[window] + dot(pair, wout_v[128:256])).astype(BF16)
@@ -770,6 +753,27 @@
         put = pltpu.make_async_copy(done.at[group_rows(frame)], res_out.at[mine], own_sem.at[1])
         put.start()
         put.wait()
+
+    def wait_stat_send(k, carry):
+        stat_copy(k).wait_send()
+        return carry
+
+    lax.fori_loop(1, n_patch, wait_stat_send, 0)
+
+    @pl.when(me < n_patch - 1)
+    def _():
+        halo_copy(0).wait_send()
+
+    @pl.when(me > 0)
+    def _():
+        halo_copy(1).wait_send()
+
+    for stage in range(2):
+        for i in range(7):
+            for direction in range(2):
+                ring_copy(stage, direction, i).wait_send()
+        query_copies[stage].wait_send()
+    store_fresh.wait()
 
     for copies in output_copies:
         for copy in copies:

time: 93.2 us -> 93.2 us (level)
  no operation moved by 1% of the time
where the time goes in v3:
time: 93.2 us; the launch traced here: 93 us
  Pallas kernels  91.6 us (98%)
  between operations  1.45 us (2%)
    pallas_call x1, Pallas kernels, body(): pl.pallas_call(functools.partial(kernel, rows, width, chans), out_shape=(...  89.5 us
    pallas_call x1, Pallas kernels, body(): pl.pallas_call(emit_kernel, out_shape=(jax.ShapeDtypeStruct((rows, chans,...  2.12 us

profile of v3, /device:TPU:1, one launch (start us, length us, event | category | flops | bytes accessed | tf_op | source)
XLA Modules:
  0.0 93.0 jit_solution(15766970558763477649)
XLA Ops:
  1.3 89.5 %layer.1 = (bf16[384,320]{1,0:T(8,128)(2,1)}, bf16[384,640]{1,0:T(8,128)(2,1)}) custom-call(bf16[3,320,128]{2,1,0:T(8,128)(2,1)} %bitcast.10, bf16[384,640]{1,0:T(8,128)(2,1)} %bitcast.9, s32[1]{0:T(128)S(6)} %copy.13.time_ref, bf16[3,3,320,320]{3,2,1,0:T(8,128)(2,1)} %conv_in.1, bf16[320,320]{1,0:T(8,128)(2,1)} %tproj_in.1, bf16[320,960]{1,0:T(8,128)(2,1)} %qkv_in.1, ...), custom_call_target="tpu_custom_call" | custom-call | tf_op jit(solution)/shard_map/layer/pallas_call | solution.py:856
  90.7 2.1 %emit.1 = (bf16[3,320,128]{2,1,0:T(8,128)(2,1)}, bf16[384,640]{1,0:T(8,128)(2,1)}) custom-call(bf16[384,320]{1,0:T(8,128)(2,1)} %get-tuple-element.6.res_in, bf16[384,640]{1,0:T(8,128)(2,1)} %get-tuple-element.7.fresh_in), custom_call_target="tpu_custom_call" | custom-call | tf_op jit(solution)/shard_map/emit/pallas_call | solution.py:933
